TPU v7x, 512 devices: a whole 4x8x8 slice. The times are simulated.
512 devices in a mesh: ctx: 64 (over z, x, y_hi), tp: 8 (over y_lo, core).
Axes of the slice: x: 4, y: 8 (y_hi: 2, y_lo: 4; y = y_hi * 4 + y_lo), z: 8, core: 2. Of those that a mesh axis runs over, the one named last changes fastest.
Arguments:
- queries: bfloat16 [16384, 4096], P('ctx', 'tp'), may hold values from -6 to 6
- keys: bfloat16 [16384, 1024], P('ctx', 'tp'), may hold values from -6 to 6
- values: bfloat16 [16384, 1024], P('ctx', 'tp'), may hold values from -6 to 6
- out_weight: bfloat16 [5120, 4096], P('ctx', 'tp'), may hold values from -0.375 to 0.375
Outputs:
- mixed: bfloat16 [16384, 5120], P('ctx', 'tp')
All inputs are finite; a program needn't handle non-finite values.
Results may differ from a plain program's by a relative error of at most 0.02.
Values may be sent and summed in bfloat16 or wider, within the bound.
A program may use at most 64 MiB of HBM per device.

v0:
```python
import math

import jax
import jax.numpy as jnp
from jax import lax
from jax.sharding import PartitionSpec as P

HD = 128


def rotate_heads(source, positions, head_count, head_width):
    half_width = head_width // 2
    frequency = jnp.exp(
        -(jnp.arange(half_width, dtype=jnp.float32) / half_width) * math.log(1000000.0)
    )
    angles = positions.astype(jnp.float32)[:, None] * frequency[None, :]
    cosine = jnp.cos(angles)[:, None, :]
    sines = jnp.sin(angles)[:, None, :]
    shaped = source.astype(jnp.float32).reshape(source.shape[0], head_count, head_width)
    first_half = shaped[:, :, :half_width]
    second_half = shaped[:, :, half_width:]
    turned = jnp.concatenate(
        [first_half * cosine - second_half * sines, second_half * cosine + first_half * sines],
        axis=2,
    )
    return turned.reshape(source.shape[0], head_count * head_width).astype(jnp.bfloat16)


def body(queries, keys, values, out_weight):
    row_count = queries.shape[0]
    ctx_place = lax.axis_index("ctx")
    head_width = HD
    query_heads = queries.shape[1] // head_width
    key_heads = keys.shape[1] // head_width
    group_size = query_heads // key_heads
    local_rows = jnp.arange(row_count, dtype=jnp.int32)
    first_rows = ctx_place * row_count + local_rows
    query_rot = rotate_heads(queries, first_rows, query_heads, head_width)
    key_rot = rotate_heads(keys, first_rows, key_heads, head_width)
    query_grid = query_rot.reshape(row_count, key_heads, group_size, head_width)
    score_scale = 1.0 / math.sqrt(head_width)
    block_rows = math.gcd(row_count, 128)
    block_count = row_count // block_rows

    def make_update(query_block, block_pos, key_piece, value_piece, key_pos):

        def update(current):
            maxima, totals, summed = current
            scores = (
                jnp.einsum(
                    "qkgd,nkd->kgqn", query_block, key_piece, preferred_element_type=jnp.float32
                )
                * score_scale
            )
            visible = key_pos[None, :] <= block_pos[:, None]
            scores = jnp.where(visible, scores, -1e30)
            new_maxima = jnp.maximum(maxima, jnp.max(scores, axis=3))
            factor = jnp.exp(maxima - new_maxima)
            unscaled = jnp.where(visible, jnp.exp(scores - new_maxima[..., None]), 0.0)
            totals = totals * factor + jnp.sum(unscaled, axis=3)
            product = jnp.einsum(
                "kgqn,nkd->kgqd",
                unscaled.astype(jnp.bfloat16),
                value_piece,
                preferred_element_type=jnp.float32,
            )
            return (new_maxima, totals, summed * factor[..., None] + product)

        return update

    initial = tuple(
        (
            (
                jnp.full((key_heads, group_size, block_rows), -1e30, jnp.float32),
                jnp.zeros((key_heads, group_size, block_rows), jnp.float32),
                jnp.zeros((key_heads, group_size, block_rows, head_width), jnp.float32),
            )
            for block_index in range(block_count)
        )
    )
    key_piece = lax.all_gather(key_rot, "ctx", axis=0, tiled=True)
    value_piece = lax.all_gather(values, "ctx", axis=0, tiled=True)
    key_rows = key_piece.shape[0]
    sub_rows = math.gcd(key_rows, 512)
    sub_count = key_rows // sub_rows
    key_stack = key_piece.reshape(sub_count, sub_rows, key_heads, head_width)
    value_stack = value_piece.reshape(sub_count, sub_rows, key_heads, head_width)

    def one_sub(states, item):
        key_shaped, value_shaped, sub_index = item
        key_pos = sub_index * sub_rows + jnp.arange(sub_rows, dtype=jnp.int32)
        earliest = jnp.min(key_pos)
        results = []
        for block_index in range(block_count):
            start = block_index * block_rows
            query_block = query_grid[start : start + block_rows]
            block_pos = first_rows[start : start + block_rows]
            update = make_update(query_block, block_pos, key_shaped, value_shaped, key_pos)
            results.append(
                lax.cond(
                    earliest > jnp.max(block_pos),
                    lambda current: current,
                    update,
                    states[block_index],
                )
            )
        return (tuple(results), None)

    final, unused = lax.scan(
        one_sub, initial, (key_stack, value_stack, jnp.arange(sub_count, dtype=jnp.int32))
    )
    states = final
    totals = jnp.concatenate([state[1] for state in states], axis=2)
    summed = jnp.concatenate([state[2] for state in states], axis=2)
    attended = (
        jnp.transpose(summed / totals[..., None], (2, 0, 1, 3))
        .reshape(row_count, -1)
        .astype(jnp.bfloat16)
    )
    partial_value = lax.dot_general(
        attended,
        lax.all_gather(out_weight, "ctx", axis=0, tiled=True),
        (((1,), (1,)), ((), ())),
        preferred_element_type=jnp.float32,
    )
    projected = lax.psum_scatter(
        partial_value.astype(jnp.bfloat16), "tp", scatter_dimension=1, tiled=True
    )
    return projected


def solution(mesh):
    placed = (P("ctx", "tp"), P("ctx", "tp"), P("ctx", "tp"), P("ctx", "tp"))
    return jax.shard_map(
        body, mesh=mesh, in_specs=placed, out_specs=P("ctx", "tp"), check_vma=False
    )
```

profile of v0, /device:TPU:6, one launch (start us, length us, event | category | flops | bytes accessed | tf_op | source)
XLA Modules:
  0.0 615.2 jit_solution(4976068066181657852)
XLA Ops:
  6.6 0.9 copy.21
  7.9 0.6 pad_maximum_fusion.1
  8.6 0.7 all-gather.5.cloned.1.call-update
  9.3 0.7 all-gather.7.cloned.1.call-update
  10.4 1.1 copy.22
  11.8 0.7 slice_reduce_fusion
  12.5 153.7 %all-gather.9.cloned.1.call-done = bf16[16384,1,128]{0,2,1:T(8,128)(2,1)} async-done(((bf16[256,1,128]{0,2,1:T(8,128)(2,1)}), bf16[16384,1,128]{0,2,1:T(8,128)(2,1)}) %all-gather.9.cloned.1.call-update) | async-done | bytes 4194320 | tf_op jit(solution)/shard_map/all_gather | solution.py:81
  166.1 6.4 %copy.29 = bf16[16384,1,128]{2,0,1:T(8,128)(2,1)} copy(bf16[16384,1,128]{0,2,1:T(8,128)(2,1)} %all-gather.9.cloned.1.call-done) | data formatting | bytes 8388608
  172.5 145.4 %all-gather.5.cloned.1.call-done = bf16[16384,128]{1,0:T(8,128)(2,1)} async-done(((bf16[256,128]{1,0:T(8,128)(2,1)}), bf16[16384,128]{1,0:T(8,128)(2,1)}) %all-gather.5.cloned.1.call-update) | async-done | bytes 4194320 | tf_op jit(solution)/shard_map/all_gather | solution.py:82
  318.0 179.4 %while.22 = (s32[]{:T(128)}, f32[1,4,128]{2,1,0:T(4,128)S(1)}, f32[1,4,128]{2,1,0:T(4,128)S(1)}, f32[1,4,128,128]{3,2,1,0:T(8,128)S(1)}, f32[1,4,128]{2,1,0:T(4,...) while((s32[]{:T(128)}, f32[1,4,128]{2,1,0:T(4,128)S(1)}, ...), condition=%wide.region_12.13_spmd.clone, body=%wide.region_2.12_spmd.clone.sunk | while | flops 273551616 | bytes 9251257 | solution.py:109
  318.0 1.0 dynamic-slice_bitcast_fusion.3
  320.3 0.6 iota_add_fusion.5
  322.1 1.2 conditional.7
  324.4 1.2 conditional.6
  325.7 1.0 dynamic-slice_bitcast_fusion.3
  327.9 0.6 iota_add_fusion.5
  329.7 1.2 conditional.7
  332.1 1.2 conditional.6
  333.3 1.0 dynamic-slice_bitcast_fusion.3
  335.5 0.6 iota_add_fusion.5
  337.3 1.2 conditional.7
  339.7 1.2 conditional.6
  340.9 1.0 dynamic-slice_bitcast_fusion.3
  343.2 0.6 iota_add_fusion.5
  345.0 1.2 conditional.7
  347.3 1.2 conditional.6
  348.6 1.0 dynamic-slice_bitcast_fusion.3
  350.8 0.6 iota_add_fusion.5
  353.9 1.0 dynamic-slice_bitcast_fusion.3
  356.1 0.6 iota_add_fusion.5
  359.2 1.0 dynamic-slice_bitcast_fusion.3
  361.4 0.6 iota_add_fusion.5
  364.5 1.0 dynamic-slice_bitcast_fusion.3
  369.8 1.0 dynamic-slice_bitcast_fusion.3
  375.1 1.0 dynamic-slice_bitcast_fusion.3
  380.4 1.0 dynamic-slice_bitcast_fusion.3
  385.8 1.0 dynamic-slice_bitcast_fusion.3
  388.0 0.6 iota_add_fusion.5
  391.1 1.0 dynamic-slice_bitcast_fusion.3
  396.4 1.0 dynamic-slice_bitcast_fusion.3
  401.7 1.0 dynamic-slice_bitcast_fusion.3
  407.0 1.0 dynamic-slice_bitcast_fusion.3
  412.3 1.1 dynamic-slice_bitcast_fusion.3
  417.8 1.0 dynamic-slice_bitcast_fusion.3
  423.1 1.0 dynamic-slice_bitcast_fusion.3
  428.4 1.0 dynamic-slice_bitcast_fusion.3
  433.7 1.0 dynamic-slice_bitcast_fusion.3
  439.0 1.0 dynamic-slice_bitcast_fusion.3
  444.3 1.0 dynamic-slice_bitcast_fusion.3
  449.6 1.0 dynamic-slice_bitcast_fusion.3
  454.9 1.0 dynamic-slice_bitcast_fusion.3
  460.2 1.0 dynamic-slice_bitcast_fusion.3
  462.5 0.6 iota_add_fusion.5
  465.6 1.0 dynamic-slice_bitcast_fusion.3
  470.9 1.0 dynamic-slice_bitcast_fusion.3
  473.1 0.6 iota_add_fusion.5
  476.2 1.0 dynamic-slice_bitcast_fusion.3
  481.5 1.0 dynamic-slice_bitcast_fusion.3
  486.8 1.0 dynamic-slice_bitcast_fusion.3
  492.1 1.0 dynamic-slice_bitcast_fusion.3
  497.8 4.1 convolution_convert_fusion
  501.9 2.6 copy.30
  504.5 102.3 %reduce-scatter.4.cloned.1.call-done = bf16[640,256]{1,0:T(8,128)(2,1)} async-done(((bf16[5120,256]{1,0:T(8,128)(2,1)}), bf16[640,256]{1,0:T(8,128)(2,1)}) %reduce-scatter.4.cloned.1.call-update) | async-done | bytes 327696
  606.8 1.9 copy.31
  (345 shorter events, 44.9 us)
Async XLA Ops:
  6.5 159.6 %all-gather.9.cloned.1.call-start = ((), (), s32[]{:S(2)}) async-start(), calls=%async_computation.3 | async-start | bytes 4259840 | tf_op jit(solution)/shard_map/all_gather | solution.py:81
  8.5 309.4 %all-gather.5.cloned.1.call-start = ((), (), s32[]{:S(2)}) async-start(), calls=%async_computation.1 | async-start | bytes 4259840 | tf_op jit(solution)/shard_map/all_gather | solution.py:82
  9.3 488.5 %all-gather.7.cloned.1.call-start = ((), (), s32[]{:S(2)}) async-start(), calls=%async_computation.2 | async-start | bytes 5324800 | tf_op jit(solution)/shard_map/all_gather | solution.py:122
  10.0 596.8 %reduce-scatter.4.cloned.1.call-start = ((), (), s32[]{:S(2)}) async-start(), calls=%async_computation.4 | async-start | bytes 2949120
Sparse Core Ops, SparseCore 0:
  11.7 154.4 all-gather.8
  170.5 147.3 all-gather.4
  322.3 156.4 all-gather.6
  504.6 102.1 reduce-scatter.3
where the time goes:
time: 618 us; the launch traced here: 615 us
  waiting for transfers between devices  403 us (65%)
  loops' own time  99.8 us (16%)
  local copies, waits for them, and re-layouts  64.4 us (10%)
  other arithmetic  24.6 us (4%)
  between operations  13.3 us (2%)
  matrix products  10.3 us (2%)
    all_gather x1, waiting for transfers between devices, body(): key_piece = lax.all_gather(key_rot, 'ctx', axis=0, tiled=True)  154 us
    all_gather x1, waiting for transfers between devices, body(): value_piece = lax.all_gather(values, 'ctx', axis=0, tiled=True)  145 us
    unnamed x5, waiting for transfers between devices  104 us
    another operation x1, loops' own time, body(): lax.scan(one_sub, initial, (key_stack, value_stack, jnp.arange(sub_count,...  97.8 us
    squeeze x32, local copies, waits for them, and re-layouts, body(): lax.scan(one_sub, initial, (key_stack, value_stack, jnp.arange(sub_count,...  31.9 us
    add x32, other arithmetic, one_sub(): key_pos = sub_index * sub_rows + jnp.arange(sub_rows, dtype=jnp.int32)  19.4 us
    dynamic_slice x32, local copies, waits for them, and re-layouts, body(): lax.scan(one_sub, initial, (key_stack, value_stack, jnp.arange(sub_count,...  18.8 us
    unnamed x6, local copies, waits for them, and re-layouts  13 us
  transfers between devices with their start and end apart: 4, of which 3 were waited for; matrix products, arithmetic and copies ran while one was open for 14% of the time, Pallas kernels for 0%

commit v1 on v0

v1 whole, which is shorter than its diff:
```python
import functools
import math

import jax
import jax.numpy as jnp
from jax import lax
from jax.experimental import pallas as pl
from jax.experimental.pallas import tpu as pltpu
from jax.sharding import PartitionSpec as P

HD = 128
NZ, NX, NH, NY, NC = 8, 4, 2, 4, 2
MESH = pl.DeviceIdType.MESH
LOW = -1e30


def rotate_heads(source, positions, head_count, head_width, scale):
    half_width = head_width // 2
    frequency = jnp.exp(
        -(jnp.arange(half_width, dtype=jnp.float32) / half_width) * math.log(1000000.0)
    )
    angles = positions.astype(jnp.float32)[:, None] * frequency[None, :]
    cosine = jnp.cos(angles)[:, None, :] * scale
    sines = jnp.sin(angles)[:, None, :] * scale
    shaped = source.astype(jnp.float32).reshape(source.shape[0], head_count, head_width)
    first_half = shaped[:, :, :half_width]
    second_half = shaped[:, :, half_width:]
    turned = jnp.concatenate(
        [first_half * cosine - second_half * sines, second_half * cosine + first_half * sines],
        axis=2,
    )
    return turned.reshape(source.shape[0], head_count * head_width).astype(jnp.bfloat16)


COUNT = 0


def numbers(*shape):
    global COUNT
    total = math.prod(shape)
    first = COUNT
    COUNT += total
    strides = [math.prod(shape[i + 1 :]) for i in range(len(shape))]
    return lambda *index: first + sum(i * s for i, s in zip(index, strides))


KV_H = numbers(1)
W_H = numbers(1)
Q_X = numbers(3)
KV_Z = numbers(2, 2, 4)
W_Z = numbers(2, 2, 4)
W_C = numbers(4)
O_X = numbers(3)
L_X = numbers(3)
A_X = numbers(3)
A_C = numbers(4)
Y_R = numbers(4, 4)
Y_L = numbers(4, 4)
F_X = numbers(3)


def kernel(
    q_ref, kv_ref, w_ref, out_ref,
    qbuf, kvbuf, wbuf, acc, mbuf, osend, orecv, lsend, lrecv, att, part,
    yleft, yright, ysend_r, ysend_l, fsend, frecv, ssem, rsem,
):
    rows = q_ref.shape[0]
    wrows = w_ref.shape[0]
    heads = q_ref.shape[1] // HD
    fw = NH * wrows
    ctx = lax.axis_index("ctx")
    tp = lax.axis_index("tp")
    z, x, h = ctx // (NX * NH), (ctx // NH) % NX, ctx % NH
    y, c = tp // NC, tp % NC

    def at(z=z, x=x, h=h, y=y, c=c):
        return (z * (NX * NH) + x * NH + h, y * NC + c)

    up, down = at(z=(z + 1) % NZ), at(z=(z + NZ - 1) % NZ)
    xs = [at(x=(x + d) % NX) for d in range(1, NX)]
    other_h, other_c = at(h=1 - h), at(c=1 - c)
    ring = h * NY + y
    y_next = (ring + 1) % (NH * NY)
    y_prev = (ring + NH * NY - 1) % (NH * NY)
    right = at(h=y_next // NY, y=y_next % NY)
    left = at(h=y_prev // NY, y=y_prev % NY)

    barrier = pltpu.get_barrier_semaphore()
    peers = [up, down, *xs, other_h, other_c, right, left]
    for peer in peers:
        pl.semaphore_signal(barrier, 1, device_id=peer, device_id_type=MESH)
    pl.semaphore_wait(barrier, len(peers))

    def copy(number, src, dst, peer):
        return pltpu.make_async_remote_copy(
            src_ref=src, dst_ref=dst, send_sem=ssem.at[number], recv_sem=rsem.at[number],
            device_id=peer, device_id_type=MESH,
        )

    sent = []

    def start(cp):
        cp.start()
        sent.append(cp)
        return cp

    def own_rows(n):
        return pl.ds(pl.multiple_of(h * n, 16), n)

    def other_rows(n):
        return pl.ds(pl.multiple_of((1 - h) * n, 16), n)

    halves = (own_rows, other_rows)

    def kv_z(direction, half, step):
        slot = (z + NZ - (step - 1)) % NZ if direction == 0 else (z + step - 1) % NZ
        ref = kvbuf.at[slot, halves[half](rows)]
        return copy(KV_Z(direction, half, step - 1), ref, ref, (up, down)[direction])

    def w_z(direction, half, step):
        slot = (z + NZ - (step - 1)) % NZ if direction == 0 else (z + step - 1) % NZ
        ref = wbuf.at[c, slot, halves[half](wrows)]
        return copy(W_Z(direction, half, step - 1), ref, ref, (up, down)[direction])

    def used(direction, half, step):
        return step <= 3 or (step == 4 and direction == half)

    kvh = start(copy(KV_H(0), kv_ref, kvbuf.at[z, own_rows(rows)], other_h))
    kvbuf[z, own_rows(rows)] = kv_ref[...]
    start(kv_z(0, 0, 1))
    start(kv_z(1, 0, 1))
    qx = [start(copy(Q_X(i), q_ref, qbuf.at[x], xs[i])) for i in (0, 2, 1)]
    wh = start(copy(W_H(0), w_ref, wbuf.at[c, z, own_rows(wrows)], other_h))
    wbuf[c, z, own_rows(wrows)] = w_ref[...]
    qbuf[x] = q_ref[...]
    acc[...] = jnp.zeros_like(acc)
    mbuf[...] = jnp.full_like(mbuf, LOW)

    def tile(place, slot, masked):
        keys = kvbuf[slot, :, 0:HD]
        vals = jnp.concatenate(
            [kvbuf[slot, :, HD : 2 * HD], jnp.ones((NH * rows, HD), jnp.bfloat16)], axis=1
        )
        for g in range(heads):
            query = qbuf[place, :, g * HD : (g + 1) * HD]
            s = lax.dot_general(
                query, keys, (((1,), (1,)), ((), ())), preferred_element_type=jnp.float32
            )
            if masked:
                key_pos = lax.broadcasted_iota(jnp.int32, s.shape, 1)
                row_pos = lax.broadcasted_iota(jnp.int32, s.shape, 0) + h * rows
                s = jnp.where(key_pos <= row_pos, s, LOW)
            old = mbuf[place, g]
            new = jnp.maximum(old, jnp.max(s, axis=1, keepdims=True))
            factor = jnp.exp2(old - new)
            p = jnp.exp2(s - jnp.concatenate([new] * (s.shape[1] // HD), axis=1))
            pv = jnp.dot(p.astype(jnp.bfloat16), vals, preferred_element_type=jnp.float32)
            mbuf[place, g] = new
            acc[place, g] = acc[place, g] * jnp.concatenate([factor] * 2, axis=1) + pv

    def attend(slot):
        @pl.loop(0, NX)
        def _(place):
            tile(place, slot, False)

    for cp in qx:
        cp.wait_recv()
    kvh.wait_recv()
    start(kv_z(0, 1, 1))
    start(kv_z(1, 1, 1))
    tile(x, z, True)

    @pl.loop(x + 1, NX)
    def _(place):
        tile(place, z, False)

    for step in range(1, 5):
        for half in range(2):
            for direction in range(2):
                if used(direction, half, step):
                    kv_z(direction, half, step).wait_recv()
                    if used(direction, half, step + 1):
                        start(kv_z(direction, half, step + 1))
        if step == 3:
            wh.wait_recv()
            for half in range(2):
                for direction in range(2):
                    start(w_z(direction, half, 1))

        @pl.when(z >= step)
        def _():
            attend((z + NZ - step) % NZ)

        if step < 4:
            @pl.when(z + step >= NZ)
            def _():
                attend((z + step) % NZ)

    def w_step(step):
        for half in range(2):
            for direction in range(2):
                if used(direction, half, step):
                    w_z(direction, half, step).wait_recv()
                    if used(direction, half, step + 1):
                        start(w_z(direction, half, step + 1))

    w_step(1)

    lane = lax.broadcasted_iota(jnp.int32, (rows, HD), 1)

    def finish(place):
        packed = jnp.full((rows, HD), LOW, jnp.float32)
        for g in range(heads):
            total = acc[place, g, :, HD : 2 * HD]
            some = total > 0.0
            safe = jnp.where(some, total, 1.0)
            osend[place, :, g * HD : (g + 1) * HD] = (
                acc[place, g, :, 0:HD] / safe
            ).astype(jnp.bfloat16)
            lse = jnp.where(some, mbuf[place, g] + jnp.log2(safe), LOW)
            packed = jnp.where(lane == g, lse, packed)
        lsend[place] = packed.T[0:8]

    ox, lx = [], []
    for d in (1, 3, 2):
        place = (x + d) % NX
        finish(place)
        ox.append(start(copy(O_X(d - 1), osend.at[place], orecv.at[x], xs[d - 1])))
        lx.append(start(copy(L_X(d - 1), lsend.at[place], lrecv.at[x], xs[d - 1])))
    finish(x)
    orecv[x] = osend[x]
    lrecv[x] = lsend[x]
    w_step(2)
    for cp in ox + lx:
        cp.wait_recv()
    lses = [lrecv[i] for i in range(NX)]
    top = functools.reduce(jnp.maximum, lses)
    shares = [jnp.exp2(v - top) for v in lses]
    whole = sum(shares)
    shares = [v / whole for v in shares]
    shares.append(jnp.zeros((HD - 8 * NX, rows), jnp.float32))
    turned = jnp.concatenate(shares, axis=0).T
    for g in range(heads):
        total = jnp.zeros((rows, HD), jnp.float32)
        for i in range(NX):
            column = turned[:, 8 * i + g : 8 * i + g + 1]
            total += column * orecv[i, :, g * HD : (g + 1) * HD].astype(jnp.float32)
        att[c, x, :, g * HD : (g + 1) * HD] = total.astype(jnp.bfloat16)

    ax = [start(copy(A_X(i), att.at[c, x], att.at[c, x], xs[i])) for i in (0, 2, 1)]
    ac = [start(copy(A_C(0), att.at[c, x], att.at[c, x], other_c))]
    w_step(3)
    w_step(4)
    wc = []
    for i in range(NZ // 2):
        ref = wbuf.at[c, 2 * i + 1 - c]
        wc.append(start(copy(W_C(i), ref, ref, other_c)))
    for n, i in enumerate((0, 2, 1)):
        ax[n].wait_recv()
        ref = att.at[c, (x + NX - 1 - i) % NX]
        ac.append(start(copy(A_C(1 + n), ref, ref, other_c)))
    for cp in ac + wc:
        cp.wait_recv()

    @pl.loop(0, NY)
    def _(dest):
        @pl.loop(0, NX)
        def _(place):
            total = jnp.zeros((fw, rows), jnp.float32)
            for col in range(NC):
                total += lax.dot_general(
                    wbuf[col, 2 * dest + c], att[col, place],
                    (((1,), (1,)), ((), ())), preferred_element_type=jnp.float32,
                )
            part[dest, place] = total

    def y_right(turn, dest):
        place = (x + 1 + turn) % NX
        return copy(
            Y_R(turn, dest), ysend_r.at[dest, place], yleft.at[dest, place], right
        )

    def y_left(turn, dest):
        place = (x + 1 + turn) % NX
        return copy(
            Y_L(turn, dest), ysend_l.at[dest, place], yright.at[dest, place], left
        )

    fx = []
    for turn in range(NX):
        place = (x + 1 + turn) % NX
        for i in range(NY - 1):
            dest = NY - 1 - i

            @pl.when(y == 0)
            def _():
                ysend_r[dest, place] = part[dest, place].astype(jnp.bfloat16)
                y_right(turn, dest).start()

            dest_l = i

            @pl.when(y == NY - 1)
            def _():
                ysend_l[dest_l, place] = part[dest_l, place].astype(jnp.bfloat16)
                y_left(turn, dest_l).start()

    for turn in range(NX):
        place = (x + 1 + turn) % NX
        for i in range(NY - 1):
            dest = NY - 1 - i

            @pl.when((y > 0) & (y < dest))
            def _():
                y_right(turn, dest).wait_recv()
                ysend_r[dest, place] = (
                    part[dest, place] + yleft[dest, place].astype(jnp.float32)
                ).astype(jnp.bfloat16)
                y_right(turn, dest).start()

            dest_l = i

            @pl.when((y < NY - 1) & (y > dest_l))
            def _():
                y_left(turn, dest_l).wait_recv()
                ysend_l[dest_l, place] = (
                    part[dest_l, place] + yright[dest_l, place].astype(jnp.float32)
                ).astype(jnp.bfloat16)
                y_left(turn, dest_l).start()

        for dest in range(NY):

            @pl.when(y == dest)
            def _():
                total = part[dest, place]
                if dest > 0:
                    y_right(turn, dest).wait_recv()
                    total += yleft[dest, place].astype(jnp.float32)
                if dest < NY - 1:
                    y_left(turn, dest).wait_recv()
                    total += yright[dest, place].astype(jnp.float32)
                fsend[place] = total.astype(jnp.bfloat16)

        if turn < NX - 1:
            fx.append(start(copy(F_X(turn), fsend.at[place], frecv.at[x], xs[turn])))
    frecv[x] = fsend[x]
    for cp in fx:
        cp.wait_recv()
    for i in range(NX):
        out_ref[i * fw : (i + 1) * fw] = frecv[i]

    for cp in sent:
        cp.wait_send()
    for turn in range(NX):
        for dest in range(NY):

            @pl.when(y < dest)
            def _():
                y_right(turn, dest).wait_send()

            @pl.when(y > dest)
            def _():
                y_left(turn, dest).wait_send()


def body(queries, keys, values, out_weight):
    rows = queries.shape[0]
    wrows = out_weight.shape[0]
    cols = queries.shape[1]
    heads = cols // HD
    fw = NH * wrows
    positions = lax.axis_index("ctx") * rows + jnp.arange(rows, dtype=jnp.int32)
    scale = math.log2(math.e) / math.sqrt(HD)
    query_rot = rotate_heads(queries, positions, heads, HD, scale)
    key_rot = rotate_heads(keys, positions, keys.shape[1] // HD, HD, 1.0)
    key_value = jnp.concatenate([key_rot, values], axis=1)
    vmem = pl.BlockSpec(memory_space=pltpu.VMEM)
    bf16, f32 = jnp.bfloat16, jnp.float32
    turned = pl.pallas_call(
        kernel,
        out_shape=jax.ShapeDtypeStruct((NX * fw, rows), bf16),
        in_specs=[vmem] * 3,
        out_specs=vmem,
        scratch_shapes=[
            pltpu.VMEM((NX, rows, cols), bf16),
            pltpu.VMEM((NZ, NH * rows, 2 * HD), bf16),
            pltpu.VMEM((NC, NZ, fw, cols), bf16),
            pltpu.VMEM((NX, heads, rows, 2 * HD), f32),
            pltpu.VMEM((NX, heads, rows, HD), f32),
            pltpu.VMEM((NX, rows, cols), bf16),
            pltpu.VMEM((NX, rows, cols), bf16),
            pltpu.VMEM((NX, 8, rows), f32),
            pltpu.VMEM((NX, 8, rows), f32),
            pltpu.VMEM((NC, NX, rows, cols), bf16),
            pltpu.VMEM((NY, NX, fw, rows), f32),
            pltpu.VMEM((NY, NX, fw, rows), bf16),
            pltpu.VMEM((NY, NX, fw, rows), bf16),
            pltpu.VMEM((NY, NX, fw, rows), bf16),
            pltpu.VMEM((NY, NX, fw, rows), bf16),
            pltpu.VMEM((NX, fw, rows), bf16),
            pltpu.VMEM((NX, fw, rows), bf16),
            pltpu.SemaphoreType.DMA((COUNT,)),
            pltpu.SemaphoreType.DMA((COUNT,)),
        ],
        compiler_params=pltpu.CompilerParams(
            collective_id=0, has_side_effects=True, vmem_limit_bytes=56 * 2**20
        ),
        name="attention_layer",
    )(query_rot, key_value, out_weight)
    return turned.T


def solution(mesh):
    placed = (P("ctx", "tp"), P("ctx", "tp"), P("ctx", "tp"), P("ctx", "tp"))
    return jax.shard_map(
        body, mesh=mesh, in_specs=placed, out_specs=P("ctx", "tp"), check_vma=False
    )
```

time: 618 us -> 138 us (0.22)
  the two profiles are of different devices: /device:TPU:6 before, /device:TPU:16 now
where the time goes in v1:
time: 138 us; the launch traced here: 137 us
  Pallas kernels  131 us (95%)
  local copies, waits for them, and re-layouts  3.99 us (3%)
  other arithmetic  2.73 us (2%)
    pallas_call x1, Pallas kernels, body(): pl.pallas_call(kernel, out_shape=jax.ShapeDtypeStruct((NX * fw, rows), bf...  131 us

profile of v1, /device:TPU:16, one launch (start us, length us, event | category | flops | bytes accessed | tf_op | source)
XLA Modules:
  0.0 137.4 jit_solution(11610333751917156867)
XLA Ops:
  0.0 0.0 copy-start
  0.0 0.5 fusion.8
  0.6 0.4 copy-done
  1.0 0.2 reshape.162
  1.1 0.5 subtract_convert_fusion
  1.6 0.4 pad_maximum_fusion
  2.0 0.0 copy-start.1
  2.0 0.7 copy.10
  2.7 0.1 copy-done.1
  2.8 0.6 fusion.5
  3.4 0.0 copy-start.2
  3.4 0.1 maximum_bitcast_fusion
  3.5 0.7 copy-done.2
  4.3 0.7 pad_maximum_fusion.1.kv_ref
  4.9 130.6 %attention_layer.1 = bf16[640,256]{1,0:T(8,128)(2,1)} custom-call(bf16[256,512]{1,0:T(8,128)(2,1)} %bitcast.11, bf16[256,256]{1,0:T(8,128)(2,1)} %pad_maximum_fusion.1.kv_ref, bf16[80,512]{1,0:T(8,128)(2,1)} %w_ref.1), custom_call_target="tpu_custom_call" | custom-call | tf_op jit(solution)/shard_map/attention_layer/pallas_call | solution.py:378
  135.6 1.9 %copy.7 = bf16[256,640]{1,0:T(8,128)(2,1)} copy(bf16[256,640]{0,1:T(8,128)(2,1)} %bitcast.10) | data formatting | bytes 655360 | tf_op jit(solution)/shard_map/transpose | solution.py:409
  (3 shorter events, 0.0 us)
Async XLA Ops:
  0.0 0.9 copy-start
  2.0 0.8 copy-start.1
  3.4 0.8 copy-start.2

commit v2 on v0

v2 whole, which is shorter than its diff:
```python
import functools
import math

import jax
import jax.numpy as jnp
from jax import lax
from jax.experimental import pallas as pl
from jax.experimental.pallas import tpu as pltpu
from jax.sharding import PartitionSpec as P

HD = 128
NZ, NX, NH, NY, NC = 8, 4, 2, 4, 2
NS = 4
NU = 2
MESH = pl.DeviceIdType.MESH
LOW = -1e30


def rotation(positions):
    half_width = HD // 2
    frequency = jnp.exp(
        -(jnp.arange(half_width, dtype=jnp.float32) / half_width) * math.log(1000000.0)
    )
    angles = positions.astype(jnp.float32)[:, None] * frequency[None, :]
    cosine = jnp.cos(angles)
    sines = jnp.sin(angles)
    return jnp.concatenate([cosine, cosine], axis=1), jnp.concatenate([-sines, sines], axis=1)


COUNT = 0


def numbers(*shape):
    global COUNT
    total = math.prod(shape)
    first = COUNT
    COUNT += total
    strides = [math.prod(shape[i + 1 :]) for i in range(len(shape))]
    return lambda *index: first + sum(i * s for i, s in zip(index, strides))


KV_H = numbers(NU)
W_H = numbers(2, 5)
Q_X = numbers(NS, 3)
KV_Z = numbers(2, 2, 4, NU)
W_Z = numbers(2, 4)
W_C = numbers(4)
O_X = numbers(NS, 3)
L_X = numbers(NS, 3)
A_X = numbers(NS, 3)
A_C = numbers(NS, 4)
Y_R = numbers(NS, 4)
Y_L = numbers(NS, 4)
F_X = numbers(NS // 2, 3)


def kernel(
    q_ref, k_ref, v_ref, w_ref, cos_ref, sin_ref, out_ref,
    qbuf, kvbuf, wbuf, acc, mbuf, osend, orecv, lsend, lrecv, att, part,
    yleft, yright, ysend_r, ysend_l, fsum, fsend, frecv, ssem, rsem,
):
    rows = q_ref.shape[0]
    wrows = w_ref.shape[0]
    heads = q_ref.shape[1] // HD
    fw = NH * wrows
    some_rows = rows // NS
    ctx = lax.axis_index("ctx")
    tp = lax.axis_index("tp")
    z, x, h = ctx // (NX * NH), (ctx // NH) % NX, ctx % NH
    y, c = tp // NC, tp % NC

    def at(z=z, x=x, h=h, y=y, c=c):
        return (z * (NX * NH) + x * NH + h, y * NC + c)

    up, down = at(z=(z + 1) % NZ), at(z=(z + NZ - 1) % NZ)
    xs = [at(x=(x + d) % NX) for d in range(1, NX)]
    other_h, other_c = at(h=1 - h), at(c=1 - c)
    ring = h * NY + y
    y_next = (ring + 1) % (NH * NY)
    y_prev = (ring + NH * NY - 1) % (NH * NY)
    right = at(h=y_next // NY, y=y_next % NY)
    left = at(h=y_prev // NY, y=y_prev % NY)

    across = at(y=(y + 2) % NY)

    barrier = pltpu.get_barrier_semaphore()
    peers = [other_h, up, down, *xs, across, right, left, other_c]
    for peer in peers:
        pl.semaphore_signal(barrier, 1, device_id=peer, device_id_type=MESH)

    def copy(number, src, dst, peer):
        return pltpu.make_async_remote_copy(
            src_ref=src, dst_ref=dst, send_sem=ssem.at[number], recv_sem=rsem.at[number],
            device_id=peer, device_id_type=MESH,
        )

    def own_rows(n):
        return pl.ds(pl.multiple_of(h * n, 16), n)

    def rotated(source):
        wide = source.astype(jnp.float32)
        return wide * cos_ref[...] + pltpu.roll(wide, HD // 2, 1) * sin_ref[...]

    def slot_of(direction, step):
        return (z + NZ - (step - 1)) % NZ if direction == 0 else (z + step - 1) % NZ

    piece = rows // NU

    def kv_rows(half, u):
        first = h * rows if half == 0 else (1 - h) * rows
        return pl.ds(pl.multiple_of(first + u * piece, piece), piece)

    def kv_h(u):
        ref = kvbuf.at[z, kv_rows(0, u)]
        return copy(KV_H(u), ref, ref, other_h)

    def kv_z(direction, half, step, u):
        ref = kvbuf.at[slot_of(direction, step), kv_rows(half, u)]
        return copy(KV_Z(direction, half, step - 1, u), ref, ref, (up, down)[direction])

    def w_z(direction, step):
        ref = wbuf.at[c, slot_of(direction, step), own_rows(wrows)]
        return copy(W_Z(direction, step - 1), ref, ref, (up, down)[direction])

    def w_h(direction, step):
        ref = wbuf.at[c, slot_of(direction, step + 1), own_rows(wrows)]
        return copy(W_H(direction, step), ref, ref, other_h)

    def w_c(i):
        ref = wbuf.at[c, 2 * i + 1 - c]
        return copy(W_C(i), ref, ref, other_c)

    def part_rows(s):
        return pl.ds(pl.multiple_of(s * some_rows, some_rows), some_rows)

    def q_x(s, i):
        ref = qbuf.at[x, part_rows(s)]
        return copy(Q_X(s, i), ref, ref, xs[i])

    def when(condition, action):
        if condition is True:
            action()
        elif condition is not False:
            pl.when(condition)(action)

    def pass_on(half, step):
        last = 4 if half == 0 else 3
        for u in range(NU):
            for direction in range(2):
                steps = last if direction == 0 else 7 - last
                here = functools.partial(kv_z, direction, half, step, u)
                there = functools.partial(kv_z, direction, half, step + 1, u)
                when(step <= steps, lambda: here().wait_recv())
                when(step < steps, lambda: there().start())

    def w_step(step):
        for direction in range(2):
            steps = 4 - direction
            when(step <= steps, lambda: w_z(direction, step).wait_recv())
            when(step < steps, lambda: w_z(direction, step + 1).start())
            when(step <= steps, lambda: w_h(direction, step).start())

    kvbuf[z, own_rows(rows), 0:HD] = rotated(k_ref[...]).astype(jnp.bfloat16)
    kvbuf[z, own_rows(rows), HD : 2 * HD] = v_ref[...]
    scale = math.log2(math.e) / math.sqrt(HD)
    for g in range(heads):
        cols = slice(g * HD, (g + 1) * HD)
        qbuf[x, :, cols] = (rotated(q_ref[:, cols]) * scale).astype(jnp.bfloat16)
    wbuf[c, z, own_rows(wrows)] = w_ref[...]
    pl.semaphore_wait(barrier, len(peers))

    for u in range(NU):
        kv_h(u).start()
    for u in range(NU):
        for direction in range(2):
            kv_z(direction, 0, 1, u).start()

    @pl.loop(0, NS)
    def _(s):
        for i in (0, 2, 1):
            q_x(s, i).start()

    w_h(0, 0).start()
    w_z(0, 1).start()
    w_z(1, 1).start()
    acc[...] = jnp.zeros_like(acc)
    mbuf[...] = jnp.full_like(mbuf, LOW)

    def tile(place, s, slots, masked):
        count = NH * rows
        query = jnp.concatenate(
            [qbuf[place, part_rows(s), g * HD : (g + 1) * HD] for g in range(heads)], axis=0
        )
        scores = []
        for slot in slots:
            scores.append(
                lax.dot_general(
                    query, kvbuf[slot, :, 0:HD],
                    (((1,), (1,)), ((), ())), preferred_element_type=jnp.float32,
                )
            )
        if masked:
            key_pos = lax.broadcasted_iota(jnp.int32, scores[0].shape, 1)
            row_pos = lax.broadcasted_iota(jnp.int32, scores[0].shape, 0) % some_rows
            seen = key_pos <= row_pos + (h * rows + s * some_rows)
            scores = [jnp.where(seen, v, LOW) for v in scores]
        old = mbuf[place, s]
        new = old
        for v in scores:
            new = jnp.maximum(new, jnp.max(v, axis=1, keepdims=True))
        factor = jnp.exp2(old - new)
        wide = jnp.concatenate([new] * (count // HD), axis=1)
        total = acc[place, s] * jnp.concatenate([factor] * 2, axis=1)
        for slot, v in zip(slots, scores):
            vals = jnp.concatenate(
                [kvbuf[slot, :, HD : 2 * HD], jnp.ones((count, HD), jnp.bfloat16)], axis=1
            )
            total += jnp.dot(
                jnp.exp2(v - wide).astype(jnp.bfloat16), vals, preferred_element_type=jnp.float32
            )
        mbuf[place, s] = new
        acc[place, s] = total

    def attend(s, step):
        lower, upper = (z + NZ - step) % NZ, (z + step) % NZ
        both = (z + step >= NZ) & (step < NZ // 2)

        @pl.when(both)
        def _():
            for place in range(NX):
                tile(place, s, (lower, upper), False)

        @pl.when(jnp.logical_not(both) & (z >= step))
        def _():
            for place in range(NX):
                tile(place, s, (lower,), False)

    pass_on(0, 1)
    for u in range(NU):
        kv_h(u).wait_recv()
        for direction in range(2):
            kv_z(direction, 1, 1, u).start()

    @pl.loop(0, NS)
    def _(s):
        for i in range(NX - 1):
            q_x(s, i).wait_recv()
        tile(x, s, (z,), True)

        @pl.loop(x + 1, NX)
        def _(place):
            tile(place, s, (z,), False)

        @pl.when(s == 1)
        def _():
            pass_on(0, 2)

    @pl.loop(1, 4)
    def _(step):
        pass_on(1, step)

        @pl.loop(0, NS)
        def _(s):
            attend(s, step)

            @pl.when((s == 0) & (step < 3))
            def _():
                pass_on(0, step + 2)

            @pl.when(s == 1)
            def _():
                w_step(step)

    pass_on(1, 4)
    w_step(4)

    def finish(place, s):
        total = acc[place, s, :, HD : 2 * HD]
        some = total > 0.0
        safe = jnp.where(some, total, 1.0)
        osend[s, place] = (acc[place, s, :, 0:HD] / safe).astype(jnp.bfloat16)
        lse = jnp.where(some, mbuf[place, s] + jnp.log2(safe), LOW)
        lsend[s, place] = lse.T[0:8]

    def l_x(s, d):
        place = (x + 1 + d) % NX
        return copy(L_X(s, d), lsend.at[s, place], lrecv.at[s, x], xs[d])

    def o_x(s, d):
        place = (x + 1 + d) % NX
        return copy(O_X(s, d), osend.at[s, place], orecv.at[s, x], xs[d])

    def send_shares(s):
        for d in (0, 2, 1):
            finish((x + 1 + d) % NX, s)
            l_x(s, d).start()
            o_x(s, d).start()
        finish(x, s)
        orecv[s, x] = osend[s, x]
        lrecv[s, x] = lsend[s, x]

    def a_x(s, i):
        ref = att.at[c, s, x]
        return copy(A_X(s, i), ref, ref, xs[i])

    def a_c(s, n):
        ref = att.at[c, s, (x + NX - n) % NX]
        return copy(A_C(s, n), ref, ref, other_c)

    def combine(s):
        for d in range(NX - 1):
            l_x(s, d).wait_recv()
            o_x(s, d).wait_recv()
        lses = [lrecv[s, i] for i in range(NX)]
        top = functools.reduce(jnp.maximum, lses)
        shares = [jnp.exp2(v - top) for v in lses]
        whole = sum(shares)
        shares = [v / whole for v in shares]
        shares.append(jnp.zeros((HD - 8 * NX, heads * some_rows), jnp.float32))
        turned = jnp.concatenate(shares, axis=0).T
        total = jnp.zeros((heads * some_rows, HD), jnp.float32)
        for i in range(NX):
            total += turned[:, 8 * i : 8 * i + 1] * orecv[s, i].astype(jnp.float32)
        total = total.astype(jnp.bfloat16)
        for g in range(heads):
            att[c, s, x, :, g * HD : (g + 1) * HD] = total[g * some_rows : (g + 1) * some_rows]
        for i in (0, 2, 1):
            a_x(s, i).start()
        a_c(s, 0).start()

    def gather(s):
        for i in (0, 2, 1):
            a_x(s, i).wait_recv()
            a_c(s, i + 1).start()

    def y_right(s, slot, peer):
        return copy(Y_R(s, slot), ysend_r.at[s, slot], yleft.at[s, slot], peer)

    def y_left(s, slot, peer):
        return copy(Y_L(s, slot), ysend_l.at[s, slot], yright.at[s, slot], peer)

    def put_right(s, slot, value, peer):
        ysend_r[s, slot] = value.astype(jnp.bfloat16)
        y_right(s, slot, peer).start()

    def put_left(s, slot, value, peer):
        ysend_l[s, slot] = value.astype(jnp.bfloat16)
        y_left(s, slot, peer).start()

    def project(s):
        for n in range(NX):
            a_c(s, n).wait_recv()
        mixed = [att[col, s].reshape(NX * some_rows, heads * HD) for col in range(NC)]

        @pl.loop(0, NY)
        def _(dest):
            total = jnp.zeros((fw, NX * some_rows), jnp.float32)
            for col in range(NC):
                total += lax.dot_general(
                    wbuf[col, 2 * dest + c], mixed[col],
                    (((1,), (1,)), ((), ())), preferred_element_type=jnp.float32,
                )
            part[s, dest] = total

        @pl.when(y == 0)
        def _():
            for dest in (3, 2, 1):
                put_right(s, dest, part[s, dest], right)

        @pl.when(y == 1)
        def _():
            put_left(s, 3, part[s, 0], left)

        @pl.when(y == 2)
        def _():
            put_right(s, 0, part[s, 3], right)

        @pl.when(y == 3)
        def _():
            for dest in (0, 1, 2):
                put_left(s, dest, part[s, dest], left)

    def sum_on(s):
        @pl.when(y == 1)
        def _():
            for dest, peer in ((3, across), (2, right)):
                y_right(s, dest, peer).wait_recv()
                put_right(s, dest, part[s, dest] + yleft[s, dest].astype(jnp.float32), peer)

        @pl.when(y == 2)
        def _():
            for dest, peer in ((0, across), (1, left)):
                y_left(s, dest, peer).wait_recv()
                put_left(s, dest, part[s, dest] + yright[s, dest].astype(jnp.float32), peer)

    def sum_up(s):
        @pl.when(y == 0)
        def _():
            y_left(s, 3, left).wait_recv()
            y_left(s, 0, across).wait_recv()
            fsum[s] = (
                part[s, 0] + yright[s, 3].astype(jnp.float32) + yright[s, 0].astype(jnp.float32)
            )

        @pl.when(y == 3)
        def _():
            y_right(s, 0, right).wait_recv()
            y_right(s, 3, across).wait_recv()
            fsum[s] = (
                part[s, 3] + yleft[s, 0].astype(jnp.float32) + yleft[s, 3].astype(jnp.float32)
            )

        for middle in (1, 2):

            @pl.when(y == middle)
            def _():
                y_right(s, middle, right).wait_recv()
                y_left(s, middle, left).wait_recv()
                fsum[s] = (
                    part[s, middle]
                    + yleft[s, middle].astype(jnp.float32)
                    + yright[s, middle].astype(jnp.float32)
                )

    def f_x(pair, d):
        place = (x + 1 + d) % NX
        return copy(F_X(pair, d), fsend.at[pair, place], frecv.at[pair, x], xs[d])

    def deliver(pair):
        first, second = fsum[2 * pair], fsum[2 * pair + 1]
        for place in range(NX):
            cols = slice(place * some_rows, (place + 1) * some_rows)
            both = jnp.concatenate([first[:, cols], second[:, cols]], axis=1)
            fsend[pair, place] = both.astype(jnp.bfloat16)
        for d in (0, 2, 1):
            f_x(pair, d).start()
        frecv[pair, x] = fsend[pair, x]

    def store(pair):
        for d in range(NX - 1):
            f_x(pair, d).wait_recv()
        whole = frecv[pair].reshape(NX * fw, 2 * some_rows).astype(jnp.float32)
        tokens = pl.ds(pl.multiple_of(pair * 2 * some_rows, 2 * some_rows), 2 * some_rows)
        out_ref[tokens] = whole.T.astype(jnp.bfloat16)

    def stage(turn, late, action, count=NS):
        pl.when((turn >= late) & (turn < late + count))(lambda: action(turn - late))

    @pl.loop(0, NS + 4)
    def _(turn):
        @pl.when(turn < NS)
        def _():
            @pl.when(z >= 4)
            def _():
                for place in range(NX):
                    tile(place, turn, ((z + NZ - 4) % NZ,), False)

            send_shares(turn)

        @pl.when(turn == 1)
        def _():
            for direction in range(2):
                for step in range(5 - direction):
                    if step > 0 or direction == 0:
                        w_h(direction, step).wait_recv()
            for i in range(NZ // 2):
                w_c(i).start()

        @pl.when(turn == 2)
        def _():
            for i in range(NZ // 2):
                w_c(i).wait_recv()

        stage(turn, 1, combine)
        stage(turn, 2, gather)
        stage(turn, 2, project)
        stage(turn, 3, sum_on)
        stage(turn, 4, sum_up)

        @pl.when((turn == 5) | (turn == 7))
        def _():
            deliver((turn - 5) // 2)

    for pair in range(NS // 2):
        store(pair)

    for u in range(NU):
        kv_h(u).wait_send()
        for direction in range(2):
            for half in range(2):
                for step in range(1, 5):
                    if step < 4 or direction == half:
                        kv_z(direction, half, step, u).wait_send()
    for direction in range(2):
        for step in range(1, 5 - direction):
            w_z(direction, step).wait_send()
        for step in range(direction, 5 - direction):
            w_h(direction, step).wait_send()
    for i in range(NZ // 2):
        w_c(i).wait_send()
    for pair in range(NS // 2):
        for d in range(NX - 1):
            f_x(pair, d).wait_send()

    @pl.loop(0, NS)
    def _(s):
        for d in range(NX - 1):
            q_x(s, d).wait_send()
            l_x(s, d).wait_send()
            o_x(s, d).wait_send()
            a_x(s, d).wait_send()
        for n in range(NX):
            a_c(s, n).wait_send()

        @pl.when(y == 0)
        def _():
            for dest in (3, 2, 1):
                y_right(s, dest, right).wait_send()

        @pl.when(y == 1)
        def _():
            y_left(s, 3, left).wait_send()
            y_right(s, 3, across).wait_send()
            y_right(s, 2, right).wait_send()

        @pl.when(y == 2)
        def _():
            y_right(s, 0, right).wait_send()
            y_left(s, 0, across).wait_send()
            y_left(s, 1, left).wait_send()

        @pl.when(y == 3)
        def _():
            for dest in (0, 1, 2):
                y_left(s, dest, left).wait_send()


def body(queries, keys, values, out_weight):
    rows = queries.shape[0]
    wrows = out_weight.shape[0]
    cols = queries.shape[1]
    heads = cols // HD
    fw = NH * wrows
    some = rows // NS
    positions = lax.axis_index("ctx") * rows + jnp.arange(rows, dtype=jnp.int32)
    cosine, sines = rotation(positions)
    vmem = pl.BlockSpec(memory_space=pltpu.VMEM)
    bf16, f32 = jnp.bfloat16, jnp.float32
    return pl.pallas_call(
        kernel,
        out_shape=jax.ShapeDtypeStruct((rows, NX * fw), bf16),
        in_specs=[vmem] * 6,
        out_specs=vmem,
        scratch_shapes=[
            pltpu.VMEM((NX, rows, cols), bf16),
            pltpu.VMEM((NZ, NH * rows, 2 * HD), bf16),
            pltpu.VMEM((NC, NZ, fw, cols), bf16),
            pltpu.VMEM((NX, NS, heads * some, 2 * HD), f32),
            pltpu.VMEM((NX, NS, heads * some, HD), f32),
            pltpu.VMEM((NS, NX, heads * some, HD), bf16),
            pltpu.VMEM((NS, NX, heads * some, HD), bf16),
            pltpu.VMEM((NS, NX, 8, heads * some), f32),
            pltpu.VMEM((NS, NX, 8, heads * some), f32),
            pltpu.VMEM((NC, NS, NX, some, cols), bf16),
            pltpu.VMEM((NS, NY, fw, NX * some), f32),
            pltpu.VMEM((NS, NY, fw, NX * some), bf16),
            pltpu.VMEM((NS, NY, fw, NX * some), bf16),
            pltpu.VMEM((NS, NY, fw, NX * some), bf16),
            pltpu.VMEM((NS, NY, fw, NX * some), bf16),
            pltpu.VMEM((NS, fw, NX * some), f32),
            pltpu.VMEM((NS // 2, NX, fw, 2 * some), bf16),
            pltpu.VMEM((NS // 2, NX, fw, 2 * some), bf16),
            pltpu.SemaphoreType.DMA((COUNT,)),
            pltpu.SemaphoreType.DMA((COUNT,)),
        ],
        compiler_params=pltpu.CompilerParams(
            collective_id=0, has_side_effects=True, vmem_limit_bytes=56 * 2**20
        ),
        name="attention_layer",
    )(queries, keys, values, out_weight, cosine, sines)


def solution(mesh):
    placed = (P("ctx", "tp"), P("ctx", "tp"), P("ctx", "tp"), P("ctx", "tp"))
    return jax.shard_map(
        body, mesh=mesh, in_specs=placed, out_specs=P("ctx", "tp"), check_vma=False
    )
```

time: 618 us -> 107 us (0.17)
  the two profiles are of different devices: /device:TPU:6 before, /device:TPU:16 now
where the time goes in v2:
time: 107 us
  Pallas kernels  104 us (97%)
  local copies, waits for them, and re-layouts  1.73 us (2%)
  other arithmetic  1.38 us (1%)
    pallas_call x1, Pallas kernels, body(): pl.pallas_call(kernel, out_shape=jax.ShapeDtypeStruct((rows, NX * fw), bf...  104 us

profile of v2, /device:TPU:16, one launch (start us, length us, event | category | flops | bytes accessed | tf_op | source)
XLA Modules:
  0.0 106.9 jit_solution(2814853614407688016)
XLA Ops:
  0.0 0.5 fusion
  0.6 0.8 pad_maximum_fusion
  1.4 103.8 %attention_layer.1 = bf16[256,640]{1,0:T(8,128)(2,1)} custom-call(bf16[256,512]{1,0:T(8,128)(2,1)} %q_ref.1, bf16[256,128]{1,0:T(8,128)(2,1)} %k_ref.1, bf16[256,128]{1,0:T(8,128)(2,1)} %v_ref.1, bf16[80,512]{1,0:T(8,128)(2,1)} %w_ref.1, f32[256,128]{1,0:T(8,128)} %get-tuple-element.8.cos_ref, f32[256,128]{1,0:T(8,128)} %get-tuple-element.9.sin_ref), custom_call_target="tpu_custom_call" | custom-call | tf_op jit(solution)/shard_map/attention_layer/pallas_call | solution.py:549
  105.2 1.7 %copy.6 = bf16[256,640]{1,0:T(8,128)(2,1)} copy(bf16[256,640]{1,0:T(8,128)(2,1)} %attention_layer.1) | data formatting | bytes 655360
  (2 shorter events, 0.0 us)

commit v3 on v2

--- a/solution.py
+++ b/solution.py
@@ -24,7 +24,7 @@
     angles = positions.astype(jnp.float32)[:, None] * frequency[None, :]
     cosine = jnp.cos(angles)
     sines = jnp.sin(angles)
-    return jnp.concatenate([cosine, cosine], axis=1), jnp.concatenate([-sines, sines], axis=1)
+    return cosine, sines
 
 
 COUNT = 0
@@ -97,9 +97,12 @@
     def own_rows(n):
         return pl.ds(pl.multiple_of(h * n, 16), n)
 
+    cosine = jnp.concatenate([cos_ref[...], cos_ref[...]], axis=1)
+    sines = jnp.concatenate([-sin_ref[...], sin_ref[...]], axis=1)
+
     def rotated(source):
         wide = source.astype(jnp.float32)
-        return wide * cos_ref[...] + pltpu.roll(wide, HD // 2, 1) * sin_ref[...]
+        return wide * cosine + pltpu.roll(wide, HD // 2, 1) * sines
 
     def slot_of(direction, step):
         return (z + NZ - (step - 1)) % NZ if direction == 0 else (z + step - 1) % NZ
@@ -118,16 +121,19 @@
         ref = kvbuf.at[slot_of(direction, step), kv_rows(half, u)]
         return copy(KV_Z(direction, half, step - 1, u), ref, ref, (up, down)[direction])
 
+    def w_at(slot):
+        return wbuf.at[c, slot % 2, slot // 2, own_rows(wrows)]
+
     def w_z(direction, step):
-        ref = wbuf.at[c, slot_of(direction, step), own_rows(wrows)]
+        ref = w_at(slot_of(direction, step))
         return copy(W_Z(direction, step - 1), ref, ref, (up, down)[direction])
 
     def w_h(direction, step):
-        ref = wbuf.at[c, slot_of(direction, step + 1), own_rows(wrows)]
+        ref = w_at(slot_of(direction, step + 1))
         return copy(W_H(direction, step), ref, ref, other_h)
 
     def w_c(i):
-        ref = wbuf.at[c, 2 * i + 1 - c]
+        ref = wbuf.at[c, 1 - c, i]
         return copy(W_C(i), ref, ref, other_c)
 
     def part_rows(s):
@@ -166,7 +172,7 @@
     for g in range(heads):
         cols = slice(g * HD, (g + 1) * HD)
         qbuf[x, :, cols] = (rotated(q_ref[:, cols]) * scale).astype(jnp.bfloat16)
-    wbuf[c, z, own_rows(wrows)] = w_ref[...]
+    wbuf[c, z % 2, z // 2, own_rows(wrows)] = w_ref[...]
     pl.semaphore_wait(barrier, len(peers))
 
     for u in range(NU):
@@ -175,19 +181,21 @@
         for direction in range(2):
             kv_z(direction, 0, 1, u).start()
 
+    w_z(0, 1).start()
+    w_z(1, 1).start()
+
     @pl.loop(0, NS)
     def _(s):
         for i in (0, 2, 1):
             q_x(s, i).start()
 
-    w_h(0, 0).start()
-    w_z(0, 1).start()
-    w_z(1, 1).start()
     acc[...] = jnp.zeros_like(acc)
     mbuf[...] = jnp.full_like(mbuf, LOW)
 
-    def tile(place, s, slots, masked):
-        count = NH * rows
+    def tile(place, s, slots, masked, half=None):
+        count = NH * rows if half is None else rows
+        first = 0 if half is None else pl.multiple_of((h if half == 0 else 1 - h) * rows, rows)
+        here = pl.ds(first, count)
         query = jnp.concatenate(
             [qbuf[place, part_rows(s), g * HD : (g + 1) * HD] for g in range(heads)], axis=0
         )
@@ -195,7 +203,7 @@
         for slot in slots:
             scores.append(
                 lax.dot_general(
-                    query, kvbuf[slot, :, 0:HD],
+                    query, kvbuf[slot, here, 0:HD],
                     (((1,), (1,)), ((), ())), preferred_element_type=jnp.float32,
                 )
             )
@@ -213,7 +221,7 @@
         total = acc[place, s] * jnp.concatenate([factor] * 2, axis=1)
         for slot, v in zip(slots, scores):
             vals = jnp.concatenate(
-                [kvbuf[slot, :, HD : 2 * HD], jnp.ones((count, HD), jnp.bfloat16)], axis=1
+                [kvbuf[slot, here, HD : 2 * HD], jnp.ones((count, HD), jnp.bfloat16)], axis=1
             )
             total += jnp.dot(
                 jnp.exp2(v - wide).astype(jnp.bfloat16), vals, preferred_element_type=jnp.float32
@@ -240,39 +248,36 @@
         kv_h(u).wait_recv()
         for direction in range(2):
             kv_z(direction, 1, 1, u).start()
+    w_h(0, 0).start()
 
     @pl.loop(0, NS)
     def _(s):
         for i in range(NX - 1):
             q_x(s, i).wait_recv()
-        tile(x, s, (z,), True)
-
-        @pl.loop(x + 1, NX)
-        def _(place):
-            tile(place, s, (z,), False)
-
-        @pl.when(s == 1)
-        def _():
-            pass_on(0, 2)
+        for own in range(NX):
+
+            @pl.when(x == own)
+            def _():
+                for place in range(own, NX):
+                    tile(place, s, (z,), place == own)
+
+        pl.when(s == 0)(lambda: w_step(1))
+        pl.when(s == 1)(lambda: pass_on(0, 2))
+        pl.when(s == 2)(lambda: pass_on(1, 1))
 
     @pl.loop(1, 4)
     def _(step):
-        pass_on(1, step)
-
         @pl.loop(0, NS)
         def _(s):
             attend(s, step)
-
-            @pl.when((s == 0) & (step < 3))
+            @pl.when((step == 3) & (z >= 4))
             def _():
-                pass_on(0, step + 2)
-
-            @pl.when(s == 1)
-            def _():
-                w_step(step)
-
-    pass_on(1, 4)
-    w_step(4)
+                for place in range(NX):
+                    tile(place, s, ((z + NZ - 4) % NZ,), False, 0)
+
+            pl.when((s == 0) & (step < 3))(lambda: pass_on(0, step + 2))
+            pl.when(s == 1)(lambda: w_step(step + 1))
+            pl.when(s == 2)(lambda: pass_on(1, step + 1))
 
     def finish(place, s):
         total = acc[place, s, :, HD : 2 * HD]
@@ -352,15 +357,13 @@
             a_c(s, n).wait_recv()
         mixed = [att[col, s].reshape(NX * some_rows, heads * HD) for col in range(NC)]
 
-        @pl.loop(0, NY)
-        def _(dest):
-            total = jnp.zeros((fw, NX * some_rows), jnp.float32)
-            for col in range(NC):
-                total += lax.dot_general(
-                    wbuf[col, 2 * dest + c], mixed[col],
-                    (((1,), (1,)), ((), ())), preferred_element_type=jnp.float32,
-                )
-            part[s, dest] = total
+        total = jnp.zeros((NY * fw, NX * some_rows), jnp.float32)
+        for col in range(NC):
+            total += lax.dot_general(
+                wbuf[col, c].reshape(NY * fw, heads * HD), mixed[col],
+                (((1,), (1,)), ((), ())), preferred_element_type=jnp.float32,
+            )
+        part[s] = total.reshape(NY, fw, NX * some_rows)
 
         @pl.when(y == 0)
         def _():
@@ -439,9 +442,8 @@
     def store(pair):
         for d in range(NX - 1):
             f_x(pair, d).wait_recv()
-        whole = frecv[pair].reshape(NX * fw, 2 * some_rows).astype(jnp.float32)
-        tokens = pl.ds(pl.multiple_of(pair * 2 * some_rows, 2 * some_rows), 2 * some_rows)
-        out_ref[tokens] = whole.T.astype(jnp.bfloat16)
+        tokens = slice(pair * 2 * some_rows, (pair + 1) * 2 * some_rows)
+        out_ref[:, tokens] = frecv[pair].reshape(NX * fw, 2 * some_rows)
 
     def stage(turn, late, action, count=NS):
         pl.when((turn >= late) & (turn < late + count))(lambda: action(turn - late))
@@ -453,9 +455,11 @@
             @pl.when(z >= 4)
             def _():
                 for place in range(NX):
-                    tile(place, turn, ((z + NZ - 4) % NZ,), False)
+                    tile(place, turn, ((z + NZ - 4) % NZ,), False, 1)
 
             send_shares(turn)
+
+        stage(turn, 1, combine)
 
         @pl.when(turn == 1)
         def _():
@@ -466,15 +470,17 @@
             for i in range(NZ // 2):
                 w_c(i).start()
 
+        stage(turn, 2, gather)
+
         @pl.when(turn == 2)
         def _():
             for i in range(NZ // 2):
                 w_c(i).wait_recv()
 
-        stage(turn, 1, combine)
-        stage(turn, 2, gather)
         stage(turn, 2, project)
+
         stage(turn, 3, sum_on)
+
         stage(turn, 4, sum_up)
 
         @pl.when((turn == 5) | (turn == 7))
@@ -546,15 +552,15 @@
     cosine, sines = rotation(positions)
     vmem = pl.BlockSpec(memory_space=pltpu.VMEM)
     bf16, f32 = jnp.bfloat16, jnp.float32
-    return pl.pallas_call(
+    turned = pl.pallas_call(
         kernel,
-        out_shape=jax.ShapeDtypeStruct((rows, NX * fw), bf16),
+        out_shape=jax.ShapeDtypeStruct((NX * fw, rows), bf16),
         in_specs=[vmem] * 6,
         out_specs=vmem,
         scratch_shapes=[
             pltpu.VMEM((NX, rows, cols), bf16),
             pltpu.VMEM((NZ, NH * rows, 2 * HD), bf16),
-            pltpu.VMEM((NC, NZ, fw, cols), bf16),
+            pltpu.VMEM((NC, 2, NZ // 2, fw, cols), bf16),
             pltpu.VMEM((NX, NS, heads * some, 2 * HD), f32),
             pltpu.VMEM((NX, NS, heads * some, HD), f32),
             pltpu.VMEM((NS, NX, heads * some, HD), bf16),
@@ -578,6 +584,7 @@
         ),
         name="attention_layer",
     )(queries, keys, values, out_weight, cosine, sines)
+    return turned.T
 
 
 def solution(mesh):

time: 107 us -> 98 us (0.916)
  the two profiles are of different devices: /device:TPU:16 before, /device:TPU:464 now
where the time goes in v3:
time: 98 us; the launch traced here: 97.8 us
  Pallas kernels  94.7 us (97%)
  local copies, waits for them, and re-layouts  1.87 us (2%)
  other arithmetic  1.25 us (1%)
    pallas_call x1, Pallas kernels, body(): pl.pallas_call(kernel, out_shape=jax.ShapeDtypeStruct((NX * fw, rows), bf...  94.7 us

profile of v3, /device:TPU:464, one launch (start us, length us, event | category | flops | bytes accessed | tf_op | source)
XLA Modules:
  0.0 97.8 jit_solution(10398816743131190423)
XLA Ops:
  0.0 1.2 %multiply_sine_fusion = (f32[256,64]{1,0:T(8,128)}, f32[256,64]{1,0:T(8,128)}) fusion(f32[64]{0:T(128)S(1)} %multiply_exponential_fusion, f32[256]{0:T(256)S(1)} %add_convert_fusion), kind=kLoop, calls=%fused_computation | loop fusion | flops 16384 | bytes 132352 | tf_op jit(solution)/shard_map/sin | solution.py:26
  1.2 94.7 %attention_layer.1 = bf16[640,256]{1,0:T(8,128)(2,1)} custom-call(bf16[256,512]{1,0:T(8,128)(2,1)} %q_ref.1, bf16[256,128]{1,0:T(8,128)(2,1)} %k_ref.1, bf16[256,128]{1,0:T(8,128)(2,1)} %v_ref.1, bf16[80,512]{1,0:T(8,128)(2,1)} %w_ref.1, f32[256,64]{1,0:T(8,128)} %get-tuple-element.6.cos_ref, f32[256,64]{1,0:T(8,128)} %get-tuple-element.5.sin_ref), custom_call_target="tpu_custom_call" | custom-call | tf_op jit(solution)/shard_map/attention_layer/pallas_call | solution.py:555
  96.0 1.9 %copy.5 = bf16[256,640]{1,0:T(8,128)(2,1)} copy(bf16[256,640]{0,1:T(8,128)(2,1)} %bitcast.1) | data formatting | bytes 655360 | tf_op jit(solution)/shard_map/transpose | solution.py:587
  (2 shorter events, 0.0 us)

commit v4 on v3

--- a/solution.py
+++ b/solution.py
@@ -229,19 +229,21 @@
         mbuf[place, s] = new
         acc[place, s] = total
 
-    def attend(s, step):
+    def attend(pair, step):
         lower, upper = (z + NZ - step) % NZ, (z + step) % NZ
         both = (z + step >= NZ) & (step < NZ // 2)
 
         @pl.when(both)
         def _():
             for place in range(NX):
-                tile(place, s, (lower, upper), False)
+                for s in range(2):
+                    tile(place, 2 * pair + s, (lower, upper), False)
 
         @pl.when(jnp.logical_not(both) & (z >= step))
         def _():
             for place in range(NX):
-                tile(place, s, (lower,), False)
+                for s in range(2):
+                    tile(place, 2 * pair + s, (lower,), False)
 
     pass_on(0, 1)
     for u in range(NU):
@@ -262,22 +264,24 @@
                     tile(place, s, (z,), place == own)
 
         pl.when(s == 0)(lambda: w_step(1))
-        pl.when(s == 1)(lambda: pass_on(0, 2))
-        pl.when(s == 2)(lambda: pass_on(1, 1))
+        pl.when(s == 2)(lambda: pass_on(0, 2))
+        pl.when(s == 3)(lambda: pass_on(1, 1))
 
     @pl.loop(1, 4)
     def _(step):
-        @pl.loop(0, NS)
-        def _(s):
-            attend(s, step)
+        @pl.loop(0, NS // 2)
+        def _(pair):
+            attend(pair, step)
+
             @pl.when((step == 3) & (z >= 4))
             def _():
                 for place in range(NX):
-                    tile(place, s, ((z + NZ - 4) % NZ,), False, 0)
-
-            pl.when((s == 0) & (step < 3))(lambda: pass_on(0, step + 2))
-            pl.when(s == 1)(lambda: w_step(step + 1))
-            pl.when(s == 2)(lambda: pass_on(1, step + 1))
+                    for s in range(2):
+                        tile(place, 2 * pair + s, ((z + NZ - 4) % NZ,), False, 0)
+
+            pl.when((pair == 0) & (step < 3))(lambda: pass_on(0, step + 2))
+            pl.when(pair == 0)(lambda: w_step(step + 1))
+            pl.when(pair == 1)(lambda: pass_on(1, step + 1))
 
     def finish(place, s):
         total = acc[place, s, :, HD : 2 * HD]
@@ -296,7 +300,7 @@
         return copy(O_X(s, d), osend.at[s, place], orecv.at[s, x], xs[d])
 
     def send_shares(s):
-        for d in (0, 2, 1):
+        for d in (1, 0, 2):
             finish((x + 1 + d) % NX, s)
             l_x(s, d).start()
             o_x(s, d).start()
@@ -329,7 +333,7 @@
         total = total.astype(jnp.bfloat16)
         for g in range(heads):
             att[c, s, x, :, g * HD : (g + 1) * HD] = total[g * some_rows : (g + 1) * some_rows]
-        for i in (0, 2, 1):
+        for i in (1, 0, 2):
             a_x(s, i).start()
         a_c(s, 0).start()
 
@@ -461,7 +465,7 @@
 
         stage(turn, 1, combine)
 
-        @pl.when(turn == 1)
+        @pl.when(turn == 2)
         def _():
             for direction in range(2):
                 for step in range(5 - direction):

time: 98 us -> 95 us (0.969)
  the two profiles are of different devices: /device:TPU:464 before, /device:TPU:16 now
where the time goes in v4:
time: 95 us; the launch traced here: 94.9 us
  Pallas kernels  91.7 us (97%)
  local copies, waits for them, and re-layouts  1.87 us (2%)
  other arithmetic  1.25 us (1%)
    pallas_call x1, Pallas kernels, body(): pl.pallas_call(kernel, out_shape=jax.ShapeDtypeStruct((NX * fw, rows), bf...  91.7 us

profile of v4, /device:TPU:16, one launch (start us, length us, event | category | flops | bytes accessed | tf_op | source)
XLA Modules:
  0.0 94.9 jit_solution(15746613280165651001)
XLA Ops:
  0.0 1.2 %multiply_sine_fusion = (f32[256,64]{1,0:T(8,128)}, f32[256,64]{1,0:T(8,128)}) fusion(f32[64]{0:T(128)S(1)} %multiply_exponential_fusion, f32[256]{0:T(256)S(1)} %add_convert_fusion), kind=kLoop, calls=%fused_computation | loop fusion | flops 16384 | bytes 132352 | tf_op jit(solution)/shard_map/sin | solution.py:26
  1.2 91.7 %attention_layer.1 = bf16[640,256]{1,0:T(8,128)(2,1)} custom-call(bf16[256,512]{1,0:T(8,128)(2,1)} %q_ref.1, bf16[256,128]{1,0:T(8,128)(2,1)} %k_ref.1, bf16[256,128]{1,0:T(8,128)(2,1)} %v_ref.1, bf16[80,512]{1,0:T(8,128)(2,1)} %w_ref.1, f32[256,64]{1,0:T(8,128)} %get-tuple-element.6.cos_ref, f32[256,64]{1,0:T(8,128)} %get-tuple-element.5.sin_ref), custom_call_target="tpu_custom_call" | custom-call | tf_op jit(solution)/shard_map/attention_layer/pallas_call | solution.py:559
  93.0 1.9 %copy.5 = bf16[256,640]{1,0:T(8,128)(2,1)} copy(bf16[256,640]{0,1:T(8,128)(2,1)} %bitcast.1) | data formatting | bytes 655360 | tf_op jit(solution)/shard_map/transpose | solution.py:591
  (2 shorter events, 0.0 us)

commit v5 on v4

--- a/solution.py
+++ b/solution.py
@@ -279,8 +279,8 @@
                     for s in range(2):
                         tile(place, 2 * pair + s, ((z + NZ - 4) % NZ,), False, 0)
 
+            pl.when(pair == 0)(lambda: w_step(step + 1))
             pl.when((pair == 0) & (step < 3))(lambda: pass_on(0, step + 2))
-            pl.when(pair == 0)(lambda: w_step(step + 1))
             pl.when(pair == 1)(lambda: pass_on(1, step + 1))
 
     def finish(place, s):

time: 95 us -> 95.1 us (level)
  no operation moved by 1% of the time
where the time goes in v5:
time: 95.1 us; the launch traced here: 94.9 us
  Pallas kernels  91.8 us (97%)
  local copies, waits for them, and re-layouts  1.87 us (2%)
  other arithmetic  1.25 us (1%)
    pallas_call x1, Pallas kernels, body(): pl.pallas_call(kernel, out_shape=jax.ShapeDtypeStruct((NX * fw, rows), bf...  91.8 us

profile of v5, /device:TPU:16, one launch (start us, length us, event | category | flops | bytes accessed | tf_op | source)
XLA Modules:
  0.0 94.9 jit_solution(352555379640727891)
XLA Ops:
  0.0 1.2 %multiply_sine_fusion = (f32[256,64]{1,0:T(8,128)}, f32[256,64]{1,0:T(8,128)}) fusion(f32[64]{0:T(128)S(1)} %multiply_exponential_fusion, f32[256]{0:T(256)S(1)} %add_convert_fusion), kind=kLoop, calls=%fused_computation | loop fusion | flops 16384 | bytes 132352 | tf_op jit(solution)/shard_map/sin | solution.py:26
  1.2 91.8 %attention_layer.1 = bf16[640,256]{1,0:T(8,128)(2,1)} custom-call(bf16[256,512]{1,0:T(8,128)(2,1)} %q_ref.1, bf16[256,128]{1,0:T(8,128)(2,1)} %k_ref.1, bf16[256,128]{1,0:T(8,128)(2,1)} %v_ref.1, bf16[80,512]{1,0:T(8,128)(2,1)} %w_ref.1, f32[256,64]{1,0:T(8,128)} %get-tuple-element.6.cos_ref, f32[256,64]{1,0:T(8,128)} %get-tuple-element.5.sin_ref), custom_call_target="tpu_custom_call" | custom-call | tf_op jit(solution)/shard_map/attention_layer/pallas_call | solution.py:559
  93.0 1.9 %copy.5 = bf16[256,640]{1,0:T(8,128)(2,1)} copy(bf16[256,640]{0,1:T(8,128)(2,1)} %bitcast.1) | data formatting | bytes 655360 | tf_op jit(solution)/shard_map/transpose | solution.py:591
  (2 shorter events, 0.0 us)
